TPU v7x, 32 devices: a whole 2x2x4 slice. The times are simulated.
32 devices in a mesh: dp: 8 (over z, x), tensor: 4 (over y, core).
Axes of the slice: x: 2, y: 2, z: 4, core: 2. Of those that a mesh axis runs over, the one named last changes fastest.
Arguments:
- tokens: bfloat16 [16384, 768], P('dp'), may hold values from -6 to 6
- lengths: int32 [16, 8], P('dp'), may hold values from 1 to 512, 1024 in all within a row
- time: int32 [16], P('dp'), may hold values from 0 to 999
- qkv_weight: bfloat16 [768, 3, 768], P(None, None, 'tensor'), may hold values from -0.21875 to 0.21875
- out_weight: bfloat16 [768, 768], P('tensor'), may hold values from -0.625 to 0.625
- up_weight: bfloat16 [768, 3072], P(None, 'tensor'), may hold values from -0.21875 to 0.21875
- up_bias: bfloat16 [3072], P('tensor'), may hold values from -3 to 3
- down_weight: bfloat16 [3072, 768], P('tensor'), may hold values from -0.109375 to 0.109375
- down_bias: bfloat16 [768], replicated, may hold values from -3 to 3
- gain_attn: bfloat16 [768], replicated, may hold values from 0.5 to 1.5
- gain_mlp: bfloat16 [768], replicated, may hold values from 0.5 to 1.5
- ada_weight: bfloat16 [128, 6, 768], replicated, may hold values from -0.5 to 0.5
- ada_bias: bfloat16 [6, 768], replicated, may hold values from -3 to 3
- cotangent: bfloat16 [16384, 768], P('dp'), may hold values from -6 to 6
Outputs:
- output: bfloat16 [16384, 768], P('dp')
- grad_tokens: bfloat16 [16384, 768], P('dp')
- grad_qkv_weight: float32 [768, 3, 768], P(None, None, 'tensor')
- grad_out_weight: float32 [768, 768], P('tensor')
- grad_up_weight: float32 [768, 3072], P(None, 'tensor')
- grad_up_bias: float32 [3072], P('tensor')
- grad_down_weight: float32 [3072, 768], P('tensor')
- grad_down_bias: float32 [768], replicated
- grad_gain_attn: float32 [768], replicated
- grad_gain_mlp: float32 [768], replicated
- grad_ada_weight: float32 [128, 6, 768], replicated
- grad_ada_bias: float32 [6, 768], replicated
Inputs may be any that keep to these rules, and one draw needn't show every extreme that they name: `lengths`: in each slot the longest document has exactly 512 tokens.
All inputs are finite; a program needn't handle non-finite values.
Results may differ from a plain program's by a relative error of at most 0.02.
Values may be sent and summed in bfloat16 or wider, within the bound.
A program may use at most 192 MiB of HBM per device.

v0:
```python
import functools
import math

import jax
import jax.numpy as jnp
import numpy as np
from jax import lax
from jax.experimental import pallas as pl
from jax.experimental.pallas import tpu as pltpu
from jax.sharding import PartitionSpec as P

HEAD_DIM = 64
HALF = HEAD_DIM // 2
EPS = 1e-05
ROWS = 256
PRECISE = lax.Precision.HIGHEST
GROUP = 16
LONGEST = 512
VMEM_LIMIT = 61 * 1024 * 1024
F32 = jnp.float32
BF16 = jnp.bfloat16
GELU_A = math.sqrt(2.0 / math.pi)
GELU_B = 0.044715

NN = (((1,), (0,)), ((), ()))
NT = (((1,), (1,)), ((), ()))
TN = (((0,), (0,)), ((), ()))


def mm(left, right, dims=NN):
    return lax.dot_general(left, right, dims, preferred_element_type=F32)


def norm_parts(v):
    center = jnp.mean(v, axis=-1, keepdims=True)
    centered = v - center
    spread = jnp.mean(centered * centered, axis=-1, keepdims=True)
    rstd = lax.rsqrt(spread + EPS)
    return centered * rstd, rstd


def only_half(block, second):
    zero = jnp.zeros_like(block)
    return jnp.concatenate([zero, block] if second else [block, zero], axis=0)


MESH = pl.DeviceIdType.MESH


def bit_of(index, bit):
    return lax.rem(index // (1 << bit), 2)


def flip(index, bit):
    return index + (1 << bit) * (1 - 2 * bit_of(index, bit))


class Reduce:
    def __init__(self, total, base, rows, inbox, inbase, order, final, send, recv, first_sem):
        self.total, self.base, self.inbox, self.send, self.recv = total, base, inbox, send, recv
        self.final = final
        self.plan, self.sem = [], first_sem
        size, halved = rows, []
        for bit in order:
            if size % 32 == 0:
                self.plan.append(("halve", bit, size // 2, inbase, list(halved)))
                size //= 2
                halved.append((bit, size))
            else:
                self.plan.append(("whole", bit, size, inbase, list(halved)))
            inbase += size
        self.inend = inbase
        while halved:
            bit, size = halved.pop()
            self.plan.append(("double", bit, size, None, list(halved)))
        self.steps = len(self.plan)
        self.turn = next((n for n, step in enumerate(self.plan) if step[0] == "double"), self.steps)

    def offset(self, halved):
        me = lax.axis_index("dp")
        at = self.base
        for bit, size in halved:
            at = at + bit_of(me, bit) * size
        return at

    def copy(self, n):
        kind, bit, size, inbase, halved = self.plan[n]
        me = lax.axis_index("dp")
        start = self.offset(halved)
        if kind == "halve":
            source = start + (1 - bit_of(me, bit)) * size
        elif kind == "whole":
            source = start
        else:
            source = start + bit_of(me, bit) * size
        origin = self.final if kind == "double" and n > self.turn else self.total
        block = pl.ds(pl.multiple_of(source, 16), size)
        return pltpu.make_async_remote_copy(
            src_ref=origin.at[block],
            dst_ref=self.final.at[block] if kind == "double" else self.inbox.at[pl.ds(inbase, size)],
            send_sem=self.send.at[self.sem + n],
            recv_sem=self.recv.at[self.sem + n],
            device_id={"dp": flip(me, bit)},
            device_id_type=MESH,
        )

    def store(self):
        at = self.offset(self.plan[self.turn - 1][4])
        kind, bit, size = self.plan[self.turn - 1][:3]
        if kind == "halve":
            at = at + bit_of(lax.axis_index("dp"), bit) * size
        block = pl.ds(pl.multiple_of(at, 16), size)
        return pltpu.make_async_copy(self.total.at[block], self.final.at[block], self.send.at[self.sem + self.steps])

    def start(self, n):
        if n < self.steps:
            self.copy(n).start()

    def finish(self, n):
        if n >= self.steps:
            return
        self.copy(n).wait()
        kind, bit, size, inbase, halved = self.plan[n]
        if kind == "double":
            if n == self.turn:
                self.store().wait()
            return
        keep = self.offset(halved)
        if kind == "halve":
            keep = keep + bit_of(lax.axis_index("dp"), bit) * size
        tile = 48 if size % 48 == 0 else 16

        @pl.loop(0, size // tile)
        def _(j):
            mine = pl.ds(pl.multiple_of(keep + j * tile, 16), tile)
            came = pl.ds(pl.multiple_of(inbase + j * tile, 16), tile)
            added = self.total[mine, :].astype(F32) + self.inbox[came, :].astype(F32)
            self.total[mine, :] = added.astype(BF16)

        if n + 1 == self.turn:
            self.store().start()
            if self.turn == self.steps:
                self.store().wait()


class Gather:
    def __init__(self, rows, dp, send, recv, first_sem):
        self.rows, self.send, self.recv, self.sem = rows, send, recv, first_sem
        self.bits = list(reversed(range(dp.bit_length() - 1))) + [None]
        self.steps = len(self.bits)

    def place(self):
        at, weight = 0, 1
        for bit in self.bits:
            index = lax.axis_index("tensor") if bit is None else lax.axis_index("dp")
            at = at + bit_of(index, bit or 0) * weight
            weight *= 2
        return at

    def own(self, row, sem):
        store = pltpu.make_async_copy(row, self.rows.at[self.place()], sem)
        store.start()
        store.wait()

    def copy(self, n):
        bit, size = self.bits[n], 1 << n
        block = self.rows.at[pl.ds((self.place() // size) * size, size)]
        axis = "tensor" if bit is None else "dp"
        return pltpu.make_async_remote_copy(
            src_ref=block,
            dst_ref=block,
            send_sem=self.send.at[self.sem + n],
            recv_sem=self.recv.at[self.sem + n],
            device_id={axis: flip(lax.axis_index(axis), bit or 0)},
            device_id_type=MESH,
        )

    def start(self, n):
        if n < self.steps:
            self.copy(n).start()

    def finish(self, n):
        if n < self.steps:
            self.copy(n).wait()


def norm_back(gn, xhat, rstd, gain):
    y = gn * gain
    mean_y = jnp.mean(y, axis=-1, keepdims=True)
    mean_yx = jnp.mean(y * xhat, axis=-1, keepdims=True)
    return rstd * (y - mean_y - xhat * mean_yx)


def col_sum(v):
    return jnp.sum(v, axis=0, keepdims=True)


class Steps:
    def __init__(self, *streams):
        self.streams, self.done = streams, [0] * len(streams)

    def start(self):
        for stream in self.streams:
            stream.start(0)

    def advance(self):
        for n, stream in enumerate(self.streams):
            if self.done[n] < stream.steps:
                stream.finish(self.done[n])
                stream.start(self.done[n] + 1)
                self.done[n] += 1

    def busy(self):
        return any(done < stream.steps for done, stream in zip(self.done, self.streams))


def block_kernel(
    dp, lengths, time, tok_h, cot_h, qkv_h, out_wh, up_h, dn_h, ada_h, gain1_i, gain2_i, bias_i, downb_i, adab_i,
    freq, inverse,
    out_h, gtok_h, gmlp_h, gatt_h, rows_h, adaw_h, totals_o,
    tok, cot, qkv_s, out_s, w_s, n2, act, pre, gml, br_own, br_par, ml_own, ml_par, gn_own, gn_par, gn1_par,
    gmid, dk, dv, gproj, qt, kt, q, k, v, att, normed, stat, cos_s, sin_s, bound, mod, small, small_par,
    box1, box2, inbox1, inbox2, vec_own, vec_par, row_own, rows_s, sums,
    load_sem, y_send, y_recv, c_send, c_recv, d_send, d_recv, o_sem,
):
    length, model = tok.shape
    local = out_wh.shape[0]
    hidden = up_h.shape[1]
    cond = freq.shape[1]
    width = 2 * local
    heads = width // HEAD_DIM
    chunks = length // ROWS
    tensor, here_dp = lax.axis_index("tensor"), lax.axis_index("dp")
    core = lax.rem(tensor, 2)
    other_core, other_y = flip(tensor, 0), flip(tensor, 1)
    bits = dp.bit_length() - 1
    scale = 1.0 / math.sqrt(HEAD_DIM)
    vt = gproj.at[pl.ds(2 * width, width)]

    barrier = pltpu.get_barrier_semaphore()
    for peer in [{"tensor": other_core}, {"tensor": other_y}] + [{"dp": flip(here_dp, b)} for b in range(bits)]:
        pl.semaphore_signal(barrier, inc=1, device_id=peer, device_id_type=MESH)

    mine_rows = pl.ds(pl.multiple_of(core * length, 16), length)
    moves = (
        (ada_h, act.at[pl.ds(0, ada_h.shape[0]), pl.ds(0, model)]),
        (tok_h.at[mine_rows], tok),
        (qkv_h, qkv_s.at[:, pl.ds(0, local)]),
        (out_wh, out_s.at[pl.ds(0, local)]),
        (up_h, w_s.at[pl.ds(0, model)]),
        (dn_h, w_s.at[pl.ds(2 * model, hidden)]),
        (cot_h.at[mine_rows], cot),
    )
    loads = [pltpu.make_async_copy(source, target, load_sem.at[n]) for n, (source, target) in enumerate(moves)]
    for load in loads:
        load.start()

    def rows_of(i):
        return pl.ds(pl.multiple_of(i * ROWS, ROWS), ROWS)

    def to_y(source, target, n):
        return pltpu.make_async_remote_copy(
            src_ref=source, dst_ref=target, send_sem=y_send.at[n], recv_sem=y_recv.at[n],
            device_id={"tensor": other_y}, device_id_type=MESH,
        )

    def to_core(source, target, n):
        return pltpu.make_async_remote_copy(
            src_ref=source, dst_ref=target, send_sem=c_send.at[n], recv_sem=c_recv.at[n],
            device_id={"tensor": other_core}, device_id_type=MESH,
        )

    def br_copy(i):
        return to_y(br_own.at[rows_of(i)], br_par.at[rows_of(i)], i)

    def gn_copy(i):
        return to_y(gn_own.at[rows_of(i)], gn_par.at[rows_of(i)], chunks + i)

    def ml_copy(i):
        return to_y(ml_own.at[rows_of(i)], ml_par.at[rows_of(i)], 2 * chunks + i)

    def gn1_copy(i):
        return to_y(n2.at[rows_of(i)], gn1_par.at[rows_of(i)], 3 * chunks + i)

    def vec_copy(n):
        return to_y(vec_own.at[n], vec_par.at[n], 4 * chunks + n)

    for n, ref in enumerate((gain1_i, gain2_i, bias_i, downb_i)):
        small[n : n + 1, : ref.shape[0]] = ref[...].astype(F32).reshape(1, ref.shape[0])
    small[4:10, :] = adab_i[...].astype(F32)
    shares = [
        to_core(qkv_h, qkv_s.at[:, pl.ds(local, local)], 0),
        to_core(out_wh, out_s.at[pl.ds(local, local)], 1),
        to_core(small, small_par, 2),
        to_core(up_h, w_s.at[pl.ds(model, model)], 3),
        to_core(dn_h, w_s.at[pl.ds(2 * model + hidden, hidden)], 4),
    ]
    pl.semaphore_wait(barrier, 2 + bits)
    for share in shares:
        share.start()

    gain1, gain2, downb = small[0:1, :], small[1:2, :], small[3:4, :]
    when = time[core].astype(F32)
    angle = jnp.broadcast_to(freq[...] * when, (8, cond))
    lane = lax.broadcasted_iota(jnp.int32, (8, cond), 1)
    feats = jnp.where(lane < cond // 2, jnp.cos(angle), jnp.sin(angle))
    high = feats.astype(BF16)
    rest = feats - high.astype(F32)
    middle_part = rest.astype(BF16)
    low_part = (rest - middle_part.astype(F32)).astype(BF16)
    sums[...] = jnp.zeros_like(sums)
    vec_own[...] = jnp.zeros_like(vec_own)
    row_own[...] = jnp.zeros_like(row_own)
    row_own[11:12, :cond] = feats[0:1, :]
    place = lax.broadcasted_iota(jnp.int32, (8, length), 1)
    start, begin, end = jnp.int32(0), jnp.zeros((8, length), jnp.int32), jnp.zeros((8, length), jnp.int32)
    for n in range(lengths.shape[1]):
        size = lengths[core, n]
        end = end + jnp.where(place >= start, size, 0)
        start = start + size
        begin = begin + jnp.where(place >= start, size, 0)
    bound[0:8, :] = begin
    bound[8:16, :] = end
    turns = inverse[...] * (place - begin)[0:1, :].astype(F32)
    cos_s[...] = jnp.cos(turns)
    sin_s[...] = jnp.sin(turns)
    loads[0].wait()
    for j in range(6):
        ada = act[j * cond : (j + 1) * cond, :model]
        vec = mm(high, ada) + mm(middle_part, ada) + mm(low_part, ada)
        mod[j : j + 1, :] = vec[0:1, :] + small[4 + j : 5 + j, :]
    for n in (1, 2):
        loads[n].wait()
    shares[0].wait()

    def project(i):
        r = rows_of(i)
        xhat, _ = norm_parts(tok[r, :].astype(F32))
        x1 = (xhat * gain1 * (1.0 + mod[1:2, :]) + mod[0:1, :]).astype(BF16)
        normed[r, :] = x1
        c, s = cos_s[:, r], sin_s[:, r]
        for part, (t_o, r_o) in enumerate(((qt, q), (kt, k), (vt, v))):
            turned = mm(qkv_s[part], x1, NT)
            if part < 2:
                pieces = []
                for h in range(heads):
                    a = turned[h * HEAD_DIM : h * HEAD_DIM + HALF]
                    b = turned[h * HEAD_DIM + HALF : (h + 1) * HEAD_DIM]
                    pieces += [a * c - b * s, b * c + a * s]
                turned = jnp.concatenate(pieces, axis=0)
            if part == 0:
                turned = turned * scale
            t_o[:, r] = turned.astype(BF16)
            r_o[r, :] = turned.T.astype(BF16)

    def allowed_keys(r, keys):
        place = lax.broadcasted_iota(jnp.int32, (keys.size, ROWS), 0) + keys.start
        return (place >= bound[0:1, r]) & (place < bound[8:9, r])

    def attend(i, keys):
        r = rows_of(i)
        allowed = allowed_keys(r, keys)
        for h in range(heads):
            pair = slice((h // 2) * 2 * HEAD_DIM, (h // 2 + 1) * 2 * HEAD_DIM)
            mine = slice(h * HEAD_DIM, (h + 1) * HEAD_DIM)
            scores = mm(k[keys, pair], only_half(qt[mine, r], h % 2))
            scores = jnp.where(allowed, scores, -1000000000.0)
            top = jnp.max(scores, axis=0, keepdims=True)
            terms = jnp.exp(scores - top)
            inv = 1.0 / jnp.sum(terms, axis=0, keepdims=True)
            att[mine, r] = (mm(vt[mine, keys], terms.astype(BF16)) * inv).astype(BF16)
            stat[h : h + 1, r] = top
            stat[8 + h : 9 + h, r] = inv
        br_own[r, :] = mm(att[:, r], out_s[...], TN).astype(BF16)
        br_copy(i).start()

    reach = min(length, ROWS + LONGEST)
    first_keys, last_keys = pl.ds(0, reach), pl.ds(length - reach, reach)

    pl.loop(0, reach // ROWS)(project)
    loads[3].wait()
    shares[1].wait()
    attend(0, first_keys)
    pl.loop(reach // ROWS, chunks)(project)

    @pl.loop(1, chunks - 1)
    def _(i):
        attend(i, pl.ds(0, length))

    attend(chunks - 1, last_keys)

    for n in (4, 5, 6):
        loads[n].wait()
    for n in (2, 3, 4):
        shares[n].wait()

    @pl.loop(0, chunks)
    def _(i):
        r = rows_of(i)
        br_copy(i).wait_recv()
        middle = tok[r, :].astype(F32) + mod[2:3, :] * (br_own[r, :].astype(F32) + br_par[r, :].astype(F32))
        xhat, _ = norm_parts(middle)
        x2 = (xhat * gain2 * (1.0 + mod[4:5, :]) + mod[3:4, :]).astype(BF16)
        n2[r, :] = x2
        grad_out = cot[r, :].astype(F32)
        g = (mod[5:6, :] * grad_out).astype(BF16)
        gml[r, :] = g
        part = jnp.zeros((ROWS, model), F32)
        grad = jnp.zeros((ROWS, model), F32)
        for n in range(2):
            up, down = w_s.at[pl.ds(n * model, model)], w_s.at[pl.ds(2 * model + n * hidden, hidden)]
            cols = slice(n * hidden, (n + 1) * hidden)
            z = mm(x2, up[...]) + (small_par if n else small)[2:3, :hidden]
            square = z * z
            t = jnp.tanh(GELU_A * z * (1.0 + GELU_B * square))
            a = (0.5 * z * (1.0 + t)).astype(BF16)
            act[r, cols] = a
            slope = 0.5 * (1.0 + t) + (0.5 * GELU_A) * z * (1.0 - t * t) * (1.0 + 3.0 * GELU_B * square)
            part = part + mm(a, down[...])
            p = (mm(g, down[...], NT) * slope).astype(BF16)
            pre[r, cols] = p
            sums[n : n + 1, :hidden] += col_sum(p.astype(F32))
            grad = grad + mm(p, up[...], NT)
        ml_own[r, :] = part.astype(BF16)
        gn_own[r, :] = grad.astype(BF16)
        vec_own[0, 0:1, :] += col_sum(grad_out * part)
        sums[2:3, :] += col_sum(grad_out)
        gn_copy(i).start()

    vec_copy(0).start()

    def up_grad(j, n):
        cols = pl.ds(pl.multiple_of(j * ROWS, ROWS), ROWS)
        return mm(n2[:, cols], pre[:, n * hidden : (n + 1) * hidden], TN)

    def down_grad(j, n):
        cols = pl.ds(pl.multiple_of(n * hidden + j * ROWS, ROWS), ROWS)
        return mm(act[:, cols], gml[...], TN)

    outbox = w_s.at[pl.ds(2 * model, model + hidden)]

    @pl.loop(0, model // ROWS)
    def _(j):
        outbox[rows_of(j), :] = up_grad(j, 1).astype(BF16)

    up_copy = to_core(outbox.at[pl.ds(0, model)], box1.at[pl.ds(0, model)], 5)
    up_copy.start()

    @pl.loop(0, hidden // ROWS)
    def _(j):
        outbox[pl.ds(pl.multiple_of(model + j * ROWS, ROWS), ROWS), :] = down_grad(j, 1).astype(BF16)

    down_copy = to_core(outbox.at[pl.ds(model, hidden)], box1.at[pl.ds(model, hidden)], 6)
    down_copy.start()
    up_copy.wait()

    @pl.loop(0, model // ROWS)
    def _(j):
        r = rows_of(j)
        w_s[r, :] = (up_grad(j, 0) + box1[r, :].astype(F32)).astype(BF16)

    order = list(range(bits))
    turned_order = order[1:2] + order[:1] + order[2:]
    orders = (order, turned_order)
    used = [0]

    def streams(total, base, rows, count, shift, inbox, inbase, final):
        made = []
        for n in range(count):
            size = rows // count
            made.append(
                Reduce(total, base + n * size, size, inbox, inbase, orders[(n + shift) % 2], final, d_send, d_recv, used[0])
            )
            inbase = made[-1].inend
            used[0] += made[-1].steps + 1
        return made, inbase

    red_up, inbase = streams(w_s, 0, model, 2, 0, inbox1, 0, gmlp_h)
    for stream in red_up:
        stream.start(0)
    down_copy.wait()

    @pl.loop(0, hidden // ROWS)
    def _(j):
        r = pl.ds(pl.multiple_of(model + j * ROWS, ROWS), ROWS)
        w_s[r, :] = (down_grad(j, 0) + box1[r, :].astype(F32)).astype(BF16)

    red_down, _ = streams(w_s, model, hidden, 2, 0, inbox1, inbase, gmlp_h)
    for stream in red_down:
        stream.start(0)
    mlp_sums = Steps(*red_up, *red_down)

    dk[...] = jnp.zeros_like(dk)
    dv[...] = jnp.zeros_like(dv)

    @pl.loop(0, chunks)
    def _(i):
        r = rows_of(i)
        gn_copy(i).wait_recv()

        @pl.when(i == chunks - 1)
        def _():
            for n in range(chunks - 1):
                ml_copy(n).start()

        branch = br_own[r, :].astype(F32) + br_par[r, :].astype(F32)
        xhat, rstd = norm_parts(tok[r, :].astype(F32) + mod[2:3, :] * branch)
        gn = gn_own[r, :].astype(F32) + gn_par[r, :].astype(F32)
        g = cot[r, :].astype(F32) + norm_back(gn, xhat, rstd, (1.0 + mod[4:5, :]) * gain2)
        gmid[r, :] = g
        sums[3:4, :] += col_sum(gn)
        sums[4:5, :] += col_sum(gn * xhat)
        sums[5:6, :] += col_sum(g * branch)
        gb = (mod[2:3, :] * g).astype(BF16)
        gml[r, :] = gb
        do_t = mm(out_s[...], gb, NT).astype(BF16)
        do = mm(gb, out_s[...], NT).astype(BF16)
        allowed = allowed_keys(r, pl.ds(0, length))
        lane = lax.broadcasted_iota(jnp.int32, (ROWS, 2 * HEAD_DIM), 1)
        c, s = cos_s[:, r], sin_s[:, r]
        for p in range(heads // 2):
            pair = slice(p * 2 * HEAD_DIM, (p + 1) * 2 * HEAD_DIM)
            dk_sum, dv_sum = dk[:, pair], dv[:, pair]
            for n in range(2):
                h = 2 * p + n
                mine = slice(h * HEAD_DIM, (h + 1) * HEAD_DIM)
                scores = mm(k[:, pair], only_half(qt[mine, r], n))
                probs = jnp.where(allowed, jnp.exp(scores - stat[h : h + 1, r]), 0.0) * stat[8 + h : 9 + h, r]
                grad_p = mm(v[:, pair], only_half(do_t[mine, :], n))
                centre = col_sum(probs * grad_p)
                grad_s = (probs * (grad_p - centre)).astype(BF16)
                dq = mm(kt[mine, :], grad_s) * scale
                ua, ub = dq[:HALF], dq[HALF:]
                gproj[h * HEAD_DIM : h * HEAD_DIM + HALF, r] = (ua * c + ub * s).astype(BF16)
                gproj[h * HEAD_DIM + HALF : (h + 1) * HEAD_DIM, r] = (ub * c - ua * s).astype(BF16)
                here = (lane >= HEAD_DIM) if n else (lane < HEAD_DIM)
                none = jnp.zeros((ROWS, 2 * HEAD_DIM), BF16)
                dk_sum = dk_sum + mm(grad_s, jnp.where(here, q[r, pair], none))
                dv_sum = dv_sum + mm(probs.astype(BF16), jnp.where(here, do[:, pair], none))
            dk[:, pair] = dk_sum
            dv[:, pair] = dv_sum
        for step, n in enumerate((chunks - 2, chunks - 1)):

            @pl.when(i == n)
            def _():
                for stream in mlp_sums.streams:
                    stream.finish(step)
                    stream.start(step + 1)

    mlp_sums.done = [2] * len(mlp_sums.streams)

    vec_copy(0).wait()
    row_own[0:1, :] = sums[3:4, :]
    row_own[1:2, :] = sums[4:5, :] * gain2
    row_own[2:3, :] = sums[5:6, :]
    row_own[3:4, :] = vec_own[0, 0:1, :] + vec_par[0, 0:1, :] + sums[2:3, :] * downb
    row_own[4:5, :] = mod[5:6, :] * sums[2:3, :]
    row_own[5:6, :] = (1.0 + mod[4:5, :]) * sums[4:5, :]
    row_own[6:7, :] = jnp.where(core == 0, sums[0:1, :], sums[1:2, :])
    row_own[7:8, :] = jnp.where(core == 0, sums[1:2, :], sums[0:1, :])
    for n in range(chunks):
        br_copy(n).wait_send()
        gn_copy(n).wait_send()

    @pl.loop(0, chunks)
    def _(i):
        r = rows_of(i)
        c, s = cos_s[:, r], sin_s[:, r]
        turned = dk[r, :].T
        pieces = []
        for h in range(heads):
            ua = turned[h * HEAD_DIM : h * HEAD_DIM + HALF]
            ub = turned[h * HEAD_DIM + HALF : (h + 1) * HEAD_DIM]
            pieces += [ua * c + ub * s, ub * c - ua * s]
        gproj[width : 2 * width, r] = jnp.concatenate(pieces, axis=0).astype(BF16)
        gproj[2 * width :, r] = dv[r, :].T.astype(BF16)

    sent2 = w_s.at[pl.ds(2 * model, 4 * local)]
    gatt = w_s.at[pl.ds(2 * model + 4 * local, 4 * local)]

    def att_grads(n):
        for part in range(3):
            rows = slice((2 * part + n) * local, (2 * part + n + 1) * local)
            yield mm(gproj[rows, :], normed[...])
        yield mm(att[n * local : (n + 1) * local, :], gml[...])

    for part, piece in enumerate(att_grads(1)):
        sent2[part * local : (part + 1) * local, :] = piece.astype(BF16)
    att_copy = to_core(sent2, box2, 7)
    att_copy.start()

    for part, piece in enumerate(att_grads(0)):
        gatt[part * local : (part + 1) * local, :] = piece.astype(BF16)
    att_copy.wait()
    for part in range(4):
        rows = slice(part * local, (part + 1) * local)
        gatt[rows, :] = (gatt[rows, :].astype(F32) + box2[rows, :].astype(F32)).astype(BF16)
    red_att, _ = streams(gatt, 0, 4 * local, 3, 1, inbox2, 0, gatt_h)
    att_sums = Steps(*red_att)
    att_sums.start()
    mlp_sums.advance()

    @pl.loop(0, chunks)
    def _(i):
        r = rows_of(i)
        gn = jnp.zeros((ROWS, model), F32)
        for part in range(3):
            gn = gn + mm(gproj[part * width : (part + 1) * width, r], qkv_s[part], TN)
        n2[r, :] = gn.astype(BF16)
        xhat, _ = norm_parts(tok[r, :].astype(F32))
        vec_own[1, 0:1, :] += col_sum(gn)
        vec_own[1, 1:2, :] += col_sum(gn * xhat)

    vec_copy(1).start()
    for n in range(chunks):
        gn1_copy(n).start()
    ml_copy(chunks - 1).start()
    slot_rows = Gather(rows_h, dp, d_send, d_recv, used[0])
    row_steps = Steps(slot_rows)

    out_copies = []

    def hand_over(source, target, i, n):
        rows = pl.ds(pl.multiple_of(core * length + i * ROWS, 16), ROWS)
        keep = pltpu.make_async_copy(source, target.at[rows], o_sem.at[n])
        give = to_core(source, target.at[rows], 8 + n)
        keep.start()
        give.start()
        out_copies.append((keep, give))

    def output_chunk(i):
        r = slice(i * ROWS, (i + 1) * ROWS)
        ml_copy(i).wait()
        middle = tok[r, :].astype(F32) + mod[2:3, :] * (br_own[r, :].astype(F32) + br_par[r, :].astype(F32))
        total = ml_own[r, :].astype(F32) + ml_par[r, :].astype(F32) + downb
        act[r, :model] = (middle + mod[5:6, :] * total).astype(BF16)
        hand_over(act.at[r, :model], out_h, i, i)

    def token_chunk(i):
        r = slice(i * ROWS, (i + 1) * ROWS)
        gn1_copy(i).wait()
        xhat, rstd = norm_parts(tok[r, :].astype(F32))
        gn = n2[r, :].astype(F32) + gn1_par[r, :].astype(F32)
        g = gmid[r, :] + norm_back(gn, xhat, rstd, (1.0 + mod[1:2, :]) * gain1)
        act[r, model : 2 * model] = g.astype(BF16)
        hand_over(act.at[r, model : 2 * model], gtok_h, i, chunks + i)

    att_sums.advance()
    output_chunk(0)
    vec_copy(1).wait()
    shift_a = vec_own[1, 0:1, :] + vec_par[1, 0:1, :]
    scale_a = vec_own[1, 1:2, :] + vec_par[1, 1:2, :]
    row_own[8:9, :] = shift_a
    row_own[9:10, :] = scale_a * gain1
    row_own[10:11, :] = (1.0 + mod[1:2, :]) * scale_a
    slot_rows.own(row_own, load_sem.at[1])
    slot_rows.start(0)
    output_chunk(1)
    mlp_sums.advance()
    att_sums.advance()
    row_steps.advance()
    for i in range(2, chunks - 1):
        output_chunk(i)
    att_sums.advance()
    row_steps.advance()
    mlp_sums.advance()
    token_chunk(0)
    att_sums.advance()
    row_steps.advance()
    token_chunk(1)
    while row_steps.busy():
        row_steps.advance()

    slots = 2 * dp
    group = min(slots, GROUP)
    totals_o[...] = jnp.zeros_like(totals_o)
    picks = ((1, 0), (1, 1), (0, 2), (0, 0), (0, 1), (0, 3))
    for first_slot in range(0, slots, group):
        take = pltpu.make_async_copy(rows_h.at[pl.ds(first_slot, group)], rows_s, load_sem.at[0])
        take.start()
        take.wait()

        def pick(n, row):
            return jnp.concatenate([rows_s[g, 8 * n + row : 8 * n + row + 1, :] for g in range(group)], axis=0)

        feat = pick(1, 3)[:, :cond]
        for j, (n, row) in enumerate(picks):
            vecs = pick(n, row)
            totals_o[j : j + 1, :] += col_sum(vecs)
            outer = lax.dot_general(feat, vecs, TN, precision=PRECISE, preferred_element_type=F32)
            rows = slice(j * cond, (j + 1) * cond)
            for side, ref in enumerate((dk, dv)):
                cut = outer[:, side * width : (side + 1) * width]
                ref[rows, :] = cut if first_slot == 0 else ref[rows, :] + cut
        totals_o[6:7, :] += col_sum(pick(1, 2))
        totals_o[7:8, :] += col_sum(pick(0, 5))
        totals_o[8:9, :] += col_sum(pick(0, 4))
        totals_o[9:10, :] += jnp.where(core == 0, col_sum(pick(0, 6)), col_sum(pick(0, 7)))
    puts = [
        pltpu.make_async_copy(
            ref.at[pl.ds(0, 6 * cond)], adaw_h.at[:, pl.ds(side * width, width)], load_sem.at[2 + side]
        )
        for side, ref in enumerate((dk, dv))
    ]
    for put in puts:
        put.start()

    att_sums.advance()
    mlp_sums.advance()
    for i in range(2, chunks - 1):
        token_chunk(i)
    att_sums.advance()
    token_chunk(chunks - 1)
    output_chunk(chunks - 1)
    while mlp_sums.busy() or att_sums.busy():
        mlp_sums.advance()
        att_sums.advance()
    for put in puts:
        put.wait()
    for keep, give in out_copies:
        keep.wait()
        give.wait()


def block_call(dp, lengths, time, hbm, small):
    tokens, _, qkv_w, out_w, up_w, down_w, ada = hbm
    slot_count, model = time.shape[0], tokens.shape[1]
    length = tokens.shape[0] // slot_count
    hidden, local = up_w.shape[1], out_w.shape[0]
    width = 2 * local
    chunks = length // ROWS
    slots = slot_count * dp
    sems = 7 * (2 * dp.bit_length()) + dp.bit_length()
    any_spec, vmem_spec = pl.BlockSpec(memory_space=pl.ANY), pl.BlockSpec(memory_space=pltpu.VMEM)
    smem_spec = pl.BlockSpec(memory_space=pltpu.SMEM)
    inbox_rows = 2 * inbox_need(dp, model // 2) + 2 * inbox_need(dp, hidden // 2)
    inbox2_rows = 3 * inbox_need(dp, 4 * local // 3)
    dma = pltpu.SemaphoreType.DMA

    def low(*shape):
        return pltpu.VMEM(shape, BF16)

    def full(*shape):
        return pltpu.VMEM(shape, F32)

    tokens_like = low(length, model)
    return pl.pallas_call(
        functools.partial(block_kernel, dp),
        in_specs=[smem_spec] * 2 + [any_spec] * len(hbm) + [vmem_spec] * len(small),
        out_specs=[any_spec] * 6 + [vmem_spec],
        out_shape=[
            jax.ShapeDtypeStruct(tokens.shape, BF16),
            jax.ShapeDtypeStruct(tokens.shape, BF16),
            jax.ShapeDtypeStruct((model + hidden, model), BF16),
            jax.ShapeDtypeStruct((4 * local, model), BF16),
            jax.ShapeDtypeStruct((slots, 16, model), F32),
            jax.ShapeDtypeStruct(ada.shape, F32),
            jax.ShapeDtypeStruct((16, model), F32),
        ],
        scratch_shapes=[
            tokens_like, tokens_like, low(3, width, model), low(width, model), low(2 * (model + hidden), model),
            tokens_like, low(length, 2 * hidden), low(length, 2 * hidden), tokens_like,
            tokens_like, tokens_like, tokens_like, tokens_like, tokens_like, tokens_like, tokens_like,
            full(length, model), full(length, width), full(length, width), low(3 * width, length),
            low(width, length), low(width, length), low(length, width), low(length, width), low(length, width),
            low(width, length), tokens_like, full(16, length), full(HALF, length), full(HALF, length),
            pltpu.VMEM((16, length), jnp.int32), full(8, model), full(16, model), full(16, model),
            low(model + hidden, model), low(4 * local, model), low(inbox_rows, model),
            low(inbox2_rows, model), full(2, 8, model), full(2, 8, model), full(16, model),
            full(min(slots, GROUP), 16, model), full(8, model),
            dma((7,)), dma((4 * chunks + 2,)), dma((4 * chunks + 2,)), dma((8 + 2 * chunks,)), dma((8 + 2 * chunks,)),
            dma((sems,)), dma((sems,)), dma((2 * chunks,)),
        ],
        compiler_params=pltpu.CompilerParams(
            collective_id=0, has_side_effects=True, vmem_limit_bytes=VMEM_LIMIT
        ),
        cost_estimate=pl.CostEstimate(flops=80_000_000_000, bytes_accessed=40_000_000, transcendentals=0),
        name="transformer_block",
    )(lengths, time, *hbm, *small)


def inbox_need(dp, rows):
    need = 0
    for _ in range(dp.bit_length() - 1):
        if rows % 32 == 0:
            rows //= 2
        need += rows
    return need


def finish_kernel(totals, *refs):
    *refs, adab_o, gain1_o, gain2_o, downb_o, upb_o = refs
    half = len(refs) // 2
    for source, target in zip(refs[:half], refs[half:]):
        target[...] = source[...].astype(target.dtype)
    adab_o[...] = totals[0:6, :]
    for n, ref in enumerate((gain1_o, gain2_o, downb_o, upb_o)):
        ref[...] = totals[6 + n : 7 + n, : ref.shape[0]].reshape(ref.shape[0])


def finish_call(totals, output, grad_tok, adaw, g_mlp, g_att, hidden, local):
    steps = 4
    model = output.shape[1]

    def rows(count, start=0):
        return pl.BlockSpec((count // steps, model), lambda i: (start * steps // count + i, 0))

    def vector(count):
        return pl.BlockSpec((count,), lambda i: (0,))

    whole = [a.shape[0] for a in (output, grad_tok, adaw)]
    parts = ((model, 0), (hidden, model), (3 * local, 0), (local, 3 * local))
    vectors = (model, model, model, hidden)
    return pl.pallas_call(
        finish_kernel,
        grid=(steps,),
        in_specs=[pl.BlockSpec(totals.shape, lambda i: (0, 0))]
        + [rows(count) for count in whole]
        + [rows(*part) for part in parts],
        out_specs=[rows(count) for count in whole]
        + [rows(count) for count, _ in parts]
        + [pl.BlockSpec((6, model), lambda i: (0, 0))]
        + [vector(count) for count in vectors],
        out_shape=[jax.ShapeDtypeStruct(a.shape, a.dtype) for a in (output, grad_tok, adaw)]
        + [jax.ShapeDtypeStruct((count, model), F32) for count, _ in parts]
        + [jax.ShapeDtypeStruct((6, model), F32)]
        + [jax.ShapeDtypeStruct((count,), F32) for count in vectors],
        compiler_params=pltpu.CompilerParams(vmem_limit_bytes=VMEM_LIMIT),
        name="grads_to_float32",
    )(totals, output, grad_tok, adaw, g_mlp, g_mlp, g_att, g_att)


def per_device(
    dp, tokens, lengths, time, qkv_weight, out_weight, up_weight, up_bias, down_weight, down_bias,
    gain_attn, gain_mlp, ada_weight, ada_bias, cotangent,
):
    model, local = tokens.shape[1], out_weight.shape[0]
    cond = ada_weight.shape[0]
    qkv = jnp.transpose(qkv_weight, (1, 2, 0))
    ada = jnp.transpose(ada_weight, (1, 0, 2)).reshape(6 * cond, model)
    half = cond // 2
    freq = np.exp(np.arange(half) * (-math.log(10000.0) / half)).astype(np.float32)
    freq = jnp.asarray(np.concatenate([freq, freq])[None])
    inverse = jnp.asarray(np.exp(np.arange(HALF) * (-2.0 * math.log(10000.0) / HEAD_DIM)).astype(np.float32)[:, None])
    output, grad_tok, g_mlp, g_att, _, g_ada, totals = block_call(
        dp, lengths, time, [tokens, cotangent, qkv, out_weight, up_weight, down_weight, ada],
        [gain_attn, gain_mlp, up_bias, down_bias, ada_bias, freq, inverse],
    )
    output, grad_tok, g_ada, g_up, g_down, g_qkv, g_out, g_adab, g_gain1, g_gain2, g_downb, g_upb = finish_call(
        totals, output, grad_tok, g_ada, g_mlp, g_att, up_bias.shape[0], local
    )
    return (
        output,
        grad_tok,
        jnp.transpose(g_qkv.reshape(3, local, model), (2, 0, 1)),
        g_out,
        g_up,
        g_upb,
        g_down,
        g_downb,
        g_gain1,
        g_gain2,
        jnp.transpose(g_ada.reshape(6, cond, model), (1, 0, 2)),
        g_adab,
    )


def solution(mesh):
    in_specs = (
        P("dp", None), P("dp", None), P("dp"), P(None, None, "tensor"), P("tensor", None), P(None, "tensor"),
        P("tensor"), P("tensor", None), P(), P(), P(), P(), P(), P("dp", None),
    )
    out_specs = (
        P("dp", None), P("dp", None), P(None, None, "tensor"), P("tensor", None), P(None, "tensor"), P("tensor"),
        P("tensor", None), P(), P(), P(), P(), P(),
    )
    return jax.shard_map(
        functools.partial(per_device, mesh.shape["dp"]),
        mesh=mesh, in_specs=in_specs, out_specs=out_specs, check_vma=False,
    )
```

profile of v0, /device:TPU:0, one launch (start us, length us, event | category | flops | bytes accessed | tf_op | source)
XLA Modules:
  0.0 182.9 jit_solution(9121371313513437778)
XLA Ops:
  0.6 172.2 %transformer_block.1 = (bf16[2048,768]{1,0:T(8,128)(2,1)}, bf16[2048,768]{1,0:T(8,128)(2,1)}, bf16[1536,768]{1,0:T(8,128)(2,1)}, bf16[768,768]{1,0:T(8,128)(2,1)...) custom-call(s32[2,8]{1,0:T(2,128)} %lengths.1, s32[2]{0:T(128)} %time.1, ...), custom_call_target="tpu_custom_call" | custom-call | flops 80000000000 | bytes 40000000 | tf_op jit(solution)/shard_map/transformer_block/pallas_call | solution.py:747
  172.9 9.8 %grads_to_float32.1 = (bf16[2048,768]{1,0:T(8,128)(2,1)}, bf16[2048,768]{1,0:T(8,128)(2,1)}, f32[768,768]{1,0:T(8,128)}, f32[768,768]{1,0:T(8,128)}, f32[768,768...) custom-call(f32[16,768]{1,0:T(8,128)} %get-tuple-element.30.totals, ...), custom_call_target="tpu_custom_call" | custom-call | tf_op jit(solution)/shard_map/grads_to_float32/pallas_call | solution.py:814
where the time goes:
time: 183 us
  Pallas kernels  182 us (99%)
    pallas_call x1, Pallas kernels, block_call(): pl.pallas_call(functools.partial(block_kernel, dp), in_specs=[smem_spec]...  172 us
    pallas_call x1, Pallas kernels, finish_call(): pl.pallas_call(finish_kernel, grid=(steps,), in_specs=[pl.BlockSpec(total...  9.83 us

commit v1 on v0

--- a/solution.py
+++ b/solution.py
@@ -128,7 +128,7 @@
         keep = self.offset(halved)
         if kind == "halve":
             keep = keep + bit_of(lax.axis_index("dp"), bit) * size
-        tile = 48 if size % 48 == 0 else 16
+        tile = next(t for t in (128, 96, 64, 48, 32, 16, size) if size % t == 0)
 
         @pl.loop(0, size // tile)
         def _(j):
@@ -539,7 +539,7 @@
                 dv_sum = dv_sum + mm(probs.astype(BF16), jnp.where(here, do[:, pair], none))
             dk[:, pair] = dk_sum
             dv[:, pair] = dv_sum
-        for step, n in enumerate((chunks - 2, chunks - 1)):
+        for step, n in enumerate((chunks - 3, chunks - 2)):
 
             @pl.when(i == n)
             def _():
@@ -588,6 +588,7 @@
         sent2[part * local : (part + 1) * local, :] = piece.astype(BF16)
     att_copy = to_core(sent2, box2, 7)
     att_copy.start()
+    mlp_sums.advance()
 
     for part, piece in enumerate(att_grads(0)):
         gatt[part * local : (part + 1) * local, :] = piece.astype(BF16)
@@ -595,10 +596,9 @@
     for part in range(4):
         rows = slice(part * local, (part + 1) * local)
         gatt[rows, :] = (gatt[rows, :].astype(F32) + box2[rows, :].astype(F32)).astype(BF16)
-    red_att, _ = streams(gatt, 0, 4 * local, 3, 1, inbox2, 0, gatt_h)
+    red_att, _ = streams(gatt, 0, 4 * local, 2, 0, inbox2, 0, gatt_h)
     att_sums = Steps(*red_att)
     att_sums.start()
-    mlp_sums.advance()
 
     @pl.loop(0, chunks)
     def _(i):
@@ -647,6 +647,7 @@
 
     att_sums.advance()
     output_chunk(0)
+    att_sums.advance()
     vec_copy(1).wait()
     shift_a = vec_own[1, 0:1, :] + vec_par[1, 0:1, :]
     scale_a = vec_own[1, 1:2, :] + vec_par[1, 1:2, :]
@@ -661,13 +662,14 @@
     row_steps.advance()
     for i in range(2, chunks - 1):
         output_chunk(i)
+    mlp_sums.advance()
     att_sums.advance()
     row_steps.advance()
-    mlp_sums.advance()
     token_chunk(0)
     att_sums.advance()
     row_steps.advance()
     token_chunk(1)
+    mlp_sums.advance()
     while row_steps.busy():
         row_steps.advance()
 
@@ -706,11 +708,8 @@
         put.start()
 
     att_sums.advance()
-    mlp_sums.advance()
-    for i in range(2, chunks - 1):
+    for i in range(2, chunks):
         token_chunk(i)
-    att_sums.advance()
-    token_chunk(chunks - 1)
     output_chunk(chunks - 1)
     while mlp_sums.busy() or att_sums.busy():
         mlp_sums.advance()
@@ -734,7 +733,7 @@
     any_spec, vmem_spec = pl.BlockSpec(memory_space=pl.ANY), pl.BlockSpec(memory_space=pltpu.VMEM)
     smem_spec = pl.BlockSpec(memory_space=pltpu.SMEM)
     inbox_rows = 2 * inbox_need(dp, model // 2) + 2 * inbox_need(dp, hidden // 2)
-    inbox2_rows = 3 * inbox_need(dp, 4 * local // 3)
+    inbox2_rows = 2 * inbox_need(dp, width)
     dma = pltpu.SemaphoreType.DMA
 
     def low(*shape):

time: 183 us -> 179 us (0.978)
  Pallas kernels: 182 us -> 178 us
    pallas_call x1, Pallas kernels: 172 us -> 168 us  [block_call(): pl.pallas_call(functools.partial(block_kernel, dp), in_specs=[smem_spec]...]
where the time goes in v1:
time: 179 us; the launch traced here: 178 us
  Pallas kernels  178 us (99%)
    pallas_call x1, Pallas kernels, block_call(): pl.pallas_call(functools.partial(block_kernel, dp), in_specs=[smem_spec]...  168 us
    pallas_call x1, Pallas kernels, finish_call(): pl.pallas_call(finish_kernel, grid=(steps,), in_specs=[pl.BlockSpec(total...  9.83 us

profile of v1, /device:TPU:0, one launch (start us, length us, event | category | flops | bytes accessed | tf_op | source)
XLA Modules:
  0.0 178.5 jit_solution(5351737665032816221)
XLA Ops:
  0.6 167.8 %transformer_block.1 = (bf16[2048,768]{1,0:T(8,128)(2,1)}, bf16[2048,768]{1,0:T(8,128)(2,1)}, bf16[1536,768]{1,0:T(8,128)(2,1)}, bf16[768,768]{1,0:T(8,128)(2,1)...) custom-call(s32[2,8]{1,0:T(2,128)} %lengths.1, s32[2]{0:T(128)} %time.1, ...), custom_call_target="tpu_custom_call" | custom-call | flops 80000000000 | bytes 40000000 | tf_op jit(solution)/shard_map/transformer_block/pallas_call | solution.py:746
  168.5 9.8 %grads_to_float32.1 = (bf16[2048,768]{1,0:T(8,128)(2,1)}, bf16[2048,768]{1,0:T(8,128)(2,1)}, f32[768,768]{1,0:T(8,128)}, f32[768,768]{1,0:T(8,128)}, f32[768,768...) custom-call(f32[16,768]{1,0:T(8,128)} %get-tuple-element.30.totals, ...), custom_call_target="tpu_custom_call" | custom-call | tf_op jit(solution)/shard_map/grads_to_float32/pallas_call | solution.py:813

commit v2 on v1

--- a/solution.py
+++ b/solution.py
@@ -646,8 +646,6 @@
         hand_over(act.at[r, model : 2 * model], gtok_h, i, chunks + i)
 
     att_sums.advance()
-    output_chunk(0)
-    att_sums.advance()
     vec_copy(1).wait()
     shift_a = vec_own[1, 0:1, :] + vec_par[1, 0:1, :]
     scale_a = vec_own[1, 1:2, :] + vec_par[1, 1:2, :]
@@ -656,6 +654,8 @@
     row_own[10:11, :] = (1.0 + mod[1:2, :]) * scale_a
     slot_rows.own(row_own, load_sem.at[1])
     slot_rows.start(0)
+    output_chunk(0)
+    att_sums.advance()
     output_chunk(1)
     mlp_sums.advance()
     att_sums.advance()
@@ -669,7 +669,6 @@
     att_sums.advance()
     row_steps.advance()
     token_chunk(1)
-    mlp_sums.advance()
     while row_steps.busy():
         row_steps.advance()
 

time: 179 us -> 178 us (level)
  Pallas kernels: 178 us -> 176 us
    pallas_call x1, Pallas kernels: 168 us -> 166 us  [block_call(): pl.pallas_call(functools.partial(block_kernel, dp), in_specs=[smem_spec]...]
where the time goes in v2:
time: 178 us; the launch traced here: 177 us
  Pallas kernels  176 us (99%)
    pallas_call x1, Pallas kernels, block_call(): pl.pallas_call(functools.partial(block_kernel, dp), in_specs=[smem_spec]...  166 us
    pallas_call x1, Pallas kernels, finish_call(): pl.pallas_call(finish_kernel, grid=(steps,), in_specs=[pl.BlockSpec(total...  9.83 us

profile of v2, /device:TPU:0, one launch (start us, length us, event | category | flops | bytes accessed | tf_op | source)
XLA Modules:
  0.0 176.5 jit_solution(444100805520275703)
XLA Ops:
  0.6 165.9 %transformer_block.1 = (bf16[2048,768]{1,0:T(8,128)(2,1)}, bf16[2048,768]{1,0:T(8,128)(2,1)}, bf16[1536,768]{1,0:T(8,128)(2,1)}, bf16[768,768]{1,0:T(8,128)(2,1)...) custom-call(s32[2,8]{1,0:T(2,128)} %lengths.1, s32[2]{0:T(128)} %time.1, ...), custom_call_target="tpu_custom_call" | custom-call | flops 80000000000 | bytes 40000000 | tf_op jit(solution)/shard_map/transformer_block/pallas_call | solution.py:745
  166.5 9.8 %grads_to_float32.1 = (bf16[2048,768]{1,0:T(8,128)(2,1)}, bf16[2048,768]{1,0:T(8,128)(2,1)}, f32[768,768]{1,0:T(8,128)}, f32[768,768]{1,0:T(8,128)}, f32[768,768...) custom-call(f32[16,768]{1,0:T(8,128)} %get-tuple-element.30.totals, ...), custom_call_target="tpu_custom_call" | custom-call | tf_op jit(solution)/shard_map/grads_to_float32/pallas_call | solution.py:812
